TPU v7x, 32 devices: a whole 2x2x4 slice. The times are simulated.
32 devices in a mesh: gx: 8 (over y, x, core), gy: 4 (over z).
Axes of the slice: x: 2, y: 2, z: 4, core: 2. Of those that a mesh axis runs over, the one named last changes fastest.
Arguments:
- tokens: bfloat16 [256, 2, 4096], P('gy', None, 'gx'), may hold values from -48 to 48
- gains: float32 [3, 4096], P(None, 'gx'), may hold values from 0.1 to 1.9
- w_qkv: bfloat16 [4096, 3, 4096], P('gx', None, 'gy'), may hold values from -0.09375 to 0.09375
- w_self_out: bfloat16 [4096, 4096], P('gy', 'gx'), may hold values from -0.09375 to 0.09375
- w_cross_q: bfloat16 [4096, 4096], P('gx', 'gy'), may hold values from -0.09375 to 0.09375
- w_cross_out: bfloat16 [4096, 4096], P('gy', 'gx'), may hold values from -0.09375 to 0.09375
- w_ffn_in: bfloat16 [4096, 2, 16384], P('gx', None, 'gy'), may hold values from -0.09375 to 0.09375
- w_ffn_out: bfloat16 [16384, 4096], P('gy', 'gx'), may hold values from -0.046875 to 0.046875
- self_keys: bfloat16 [256, 32, 4096], P(('gx', 'gy')), may hold values from -6 to 6
- self_values: bfloat16 [256, 32, 4096], P(('gx', 'gy')), may hold values from -6 to 6
- cross_keys: bfloat16 [256, 128, 4096], P(('gx', 'gy')), may hold values from -6 to 6
- cross_values: bfloat16 [256, 128, 4096], P(('gx', 'gy')), may hold values from -6 to 6
- positions: int32 [256], P(('gx', 'gy')), may hold values from 1 to 32
- src_len: int32 [256], P(('gx', 'gy')), may hold values from 1 to 128, 20480 in all
Outputs:
- layer_out: bfloat16 [256, 2, 4096], P('gy', None, 'gx')
Inputs may be any that keep to these rules, and one draw needn't show every extreme that they name: `positions`: the number of filled cache slots of a row; the row's new tokens follow them. `src_len`: some row has exactly 128 source positions.
All inputs are finite; a program needn't handle non-finite values. No bound on the sum of `src_len` on one device may be relied on, other than what follows from the above.
Results may differ from a plain program's by a relative error of at most 0.023.
Values may be sent and summed in bfloat16 or wider, within the bound.
A program may use at most 192 MiB of HBM per device.

v0:
```python
import jax
import jax.numpy as jnp
from jax import lax
from jax.sharding import PartitionSpec as P

D = 4096
HEAD_DIM = 256
NEW = 2


EPSILON = 1e-06


def gather_in(stream, gain_row, weight):
    widened = lax.all_gather(stream, "gy", axis=0, tiled=True).astype(jnp.float32)
    squares = jnp.sum(widened * widened, axis=-1)
    scaled = (widened * gain_row).astype(jnp.bfloat16)
    product = lax.dot_general(
        scaled, weight, (((2,), (0,)), ((), ())), preferred_element_type=jnp.float32
    )
    return (product, squares)


def combine_rows(partials):
    return (
        lax.psum_scatter(
            partials[0].astype(jnp.bfloat16), "gx", scatter_dimension=0, tiled=True
        ).astype(jnp.float32),
        lax.psum_scatter(
            partials[1].astype(jnp.bfloat16), "gx", scatter_dimension=0, tiled=True
        ).astype(jnp.float32),
    )


def regroup(blocks):
    return lax.all_to_all(blocks, "gy", split_axis=0, concat_axis=0, tiled=True)


def project_out(activity, weight):
    return lax.dot_general(
        lax.all_gather(activity, "gx", axis=0, tiled=True),
        weight,
        (((2,), (0,)), ((), ())),
        preferred_element_type=jnp.float32,
    )


def sum_out(partials):
    return lax.psum_scatter(
        partials.astype(jnp.bfloat16), "gy", scatter_dimension=0, tiled=True
    ).astype(jnp.float32)


def self_attend(queries, new_keys, new_values, cached_keys, cached_values, positions):
    score_scale = HEAD_DIM ** (-0.5)
    scores = (
        jnp.einsum("grshd,rlghd->rghsl", queries, cached_keys, preferred_element_type=jnp.float32)
        * score_scale
    )
    visible = jnp.arange(cached_keys.shape[1])[None, :] < positions[:, None]
    cached_exp = jnp.where(visible[:, None, None, None, :], jnp.exp(scores), 0.0)
    fresh = (
        jnp.einsum("grshd,grthd->rghst", queries, new_keys, preferred_element_type=jnp.float32)
        * score_scale
    )
    causal = jnp.arange(NEW)[None, :] <= jnp.arange(NEW)[:, None]
    fresh_exp = jnp.where(causal, jnp.exp(fresh), 0.0)
    totals = jnp.sum(cached_exp, -1) + jnp.sum(fresh_exp, -1)
    cached_weights = (cached_exp / totals[..., None]).astype(jnp.bfloat16)
    fresh_weights = (fresh_exp / totals[..., None]).astype(jnp.bfloat16)
    attended = jnp.einsum(
        "rghsl,rlghd->grshd", cached_weights, cached_values, preferred_element_type=jnp.float32
    )
    attended = attended + jnp.einsum(
        "rghst,grthd->grshd", fresh_weights, new_values, preferred_element_type=jnp.float32
    )
    return attended.astype(jnp.bfloat16)


def cross_attend(queries, cached_keys, cached_values, lengths):
    score_scale = HEAD_DIM ** (-0.5)
    scores = (
        jnp.einsum("grshd,rlghd->rghsl", queries, cached_keys, preferred_element_type=jnp.float32)
        * score_scale
    )
    visible = jnp.arange(cached_keys.shape[1])[None, :] < lengths[:, None]
    source_exp = jnp.where(visible[:, None, None, None, :], jnp.exp(scores), 0.0)
    totals = jnp.sum(source_exp, -1)
    weights = (source_exp / totals[..., None]).astype(jnp.bfloat16)
    attended = jnp.einsum(
        "rghsl,rlghd->grshd", weights, cached_values, preferred_element_type=jnp.float32
    )
    return attended.astype(jnp.bfloat16)


def factor_of(squares):
    return lax.rsqrt(squares / D + EPSILON)


def per_device(
    tokens,
    gains,
    w_qkv,
    w_self_out,
    w_cross_q,
    w_cross_out,
    w_ffn_in,
    w_ffn_out,
    self_keys,
    self_values,
    cross_keys,
    cross_values,
    positions,
    src_len,
):
    groups = lax.axis_size("gy")
    rows_dev = self_keys.shape[0]
    heads_local = w_qkv.shape[2] // HEAD_DIM
    cache_slots = self_keys.shape[1]
    source_slots = cross_keys.shape[1]
    summed, squares = combine_rows(gather_in(tokens, gains[0], w_qkv))
    projected = (summed * factor_of(squares)[:, :, None, None]).astype(jnp.bfloat16)
    projected = regroup(projected.reshape(groups, rows_dev, NEW, 3, heads_local, HEAD_DIM))
    key_cache = self_keys.reshape(rows_dev, cache_slots, groups, heads_local, HEAD_DIM)
    value_cache = self_values.reshape(rows_dev, cache_slots, groups, heads_local, HEAD_DIM)
    attended = self_attend(
        projected[:, :, :, 0],
        projected[:, :, :, 1],
        projected[:, :, :, 2],
        key_cache,
        value_cache,
        positions,
    )
    attended = regroup(attended).reshape(groups * rows_dev, NEW, heads_local * HEAD_DIM)
    after_self = (tokens.astype(jnp.float32) + sum_out(project_out(attended, w_self_out))).astype(
        jnp.bfloat16
    )
    summed, squares = combine_rows(gather_in(after_self, gains[1], w_cross_q))
    cross_queries = (summed * factor_of(squares)[:, :, None]).astype(jnp.bfloat16)
    cross_queries = regroup(cross_queries.reshape(groups, rows_dev, NEW, heads_local, HEAD_DIM))
    source_keys = cross_keys.reshape(rows_dev, source_slots, groups, heads_local, HEAD_DIM)
    source_values = cross_values.reshape(rows_dev, source_slots, groups, heads_local, HEAD_DIM)
    crossed = cross_attend(cross_queries, source_keys, source_values, src_len)
    crossed = regroup(crossed).reshape(groups * rows_dev, NEW, heads_local * HEAD_DIM)
    after_cross = (
        after_self.astype(jnp.float32) + sum_out(project_out(crossed, w_cross_out))
    ).astype(jnp.bfloat16)
    ffn_partials = gather_in(after_cross, gains[2], w_ffn_in)
    summed, squares = (
        lax.psum(ffn_partials[0].astype(jnp.bfloat16), "gx").astype(jnp.float32),
        lax.psum(ffn_partials[1].astype(jnp.bfloat16), "gx").astype(jnp.float32),
    )
    gate_up = summed * factor_of(squares)[:, :, None, None]
    hidden = (jax.nn.silu(gate_up[:, :, 0]) * gate_up[:, :, 1]).astype(jnp.bfloat16)
    partials = lax.dot_general(
        hidden, w_ffn_out, (((2,), (0,)), ((), ())), preferred_element_type=jnp.float32
    )
    return (after_cross.astype(jnp.float32) + sum_out(partials)).astype(jnp.bfloat16)


def solution(mesh):
    return jax.shard_map(
        per_device,
        mesh=mesh,
        in_specs=(
            P("gy", None, "gx"),
            P(None, "gx"),
            P("gx", None, "gy"),
            P("gy", "gx"),
            P("gx", "gy"),
            P("gy", "gx"),
            P("gx", None, "gy"),
            P("gy", "gx"),
            P(("gx", "gy"), None, None),
            P(("gx", "gy"), None, None),
            P(("gx", "gy"), None, None),
            P(("gx", "gy"), None, None),
            P(("gx", "gy")),
            P(("gx", "gy")),
        ),
        out_specs=P("gy", None, "gx"),
        check_vma=False,
    )
```

profile of v0, /device:TPU:7, one launch (start us, length us, event | category | flops | bytes accessed | tf_op | source)
XLA Modules:
  0.0 574.0 jit_solution(4606593964344950288)
XLA Ops:
  6.5 14.8 %all_gather.15 = bf16[256,2,512]{2,1,0:T(2,128)(2,1)S(1)} all-gather(bf16[64,2,512]{2,1,0:T(2,128)(2,1)} %param.14), channel_id=1, replica_groups=mesh['gx'=8,'gy'=4] {'gy'}, dimensions={0}, use_global_device_ids=true | all-gather | bytes 655360 | tf_op jit(solution)/shard_map/all_gather | solution.py:15
  24.0 4.5 fusion.17
  28.5 29.7 %reduce-scatter.22.cloned.1.call-done = bf16[32,2]{1,0:T(8,128)(2,1)} async-done(((bf16[256,2]{1,0:T(8,128)(2,1)}), bf16[32,2]{1,0:T(8,128)(2,1)}) %reduce-scatter.22.cloned.1.call-update) | async-done | bytes 144
  59.0 49.7 %reduce-scatter.12.cloned.1.call-done = bf16[32,2,3,1024]{3,0,2,1:T(8,128)(2,1)} async-done(((bf16[256,2,3,1024]{3,0,2,1:T(8,128)(2,1)}), bf16[32,2,3,1024]{3,0,2,1:T(8,128)(2,1)}) %reduce-scatter.12.cloned.1.call-update) | async-done | bytes 393232 | tf_op jit(solution)/shard_map/reduce_scatter | solution.py:26
  111.0 4.3 all-to-all-start
  115.3 4.5 reshape.71
  119.8 2.8 reshape.72
  122.7 3.6 all-to-all-done
  130.4 2.4 fusion.35
  132.9 7.1 %all_to_all.20 = bf16[4,8,2,4,256]{4,2,3,1,0:T(2,128)(2,1)S(1)} all-to-all(bf16[4,8,2,4,256]{4,2,3,1,0:T(2,128)(2,1)S(1)} %fusion.35), channel_id=1, replica_groups=mesh['gx'=8,'gy'=4] {'gy'}, dimensions={0} | all-to-all | bytes 262144 | tf_op jit(solution)/shard_map/all_to_all | solution.py:36
  140.9 24.5 %all-gather.3.cloned.1.call-done = bf16[256,2,1024]{2,0,1:T(8,128)(2,1)} async-done(((bf16[32,2,1024]{2,0,1:T(8,128)(2,1)}), bf16[256,2,1024]{2,0,1:T(8,128)(2,1)}) %all-gather.3.cloned.1.call-update) | async-done | bytes 1048592 | tf_op jit(solution)/shard_map/all_gather | solution.py:41
  165.3 2.7 convolution_convert_fusion.2
  168.1 20.5 %reduce-scatter.14.cloned.1.call-done = bf16[64,2,512]{2,0,1:T(8,128)(2,1)} async-done(((bf16[256,2,512]{2,0,1:T(8,128)(2,1)}), bf16[64,2,512]{2,0,1:T(8,128)(2,1)}) %reduce-scatter.14.cloned.1.call-update) | async-done | bytes 131088 | tf_op jit(solution)/shard_map/reduce_scatter | solution.py:49
  189.6 12.9 %all_gather.17 = bf16[256,2,512]{2,0,1:T(8,128)(2,1)S(1)} all-gather(bf16[64,2,512]{2,0,1:T(8,128)(2,1)S(1)} %add_convert_fusion.2), channel_id=1, replica_groups=mesh['gx'=8,'gy'=4] {'gy'}, dimensions={0}, use_global_device_ids=true | all-gather | bytes 655360 | tf_op jit(solution)/shard_map/all_gather | solution.py:15
  205.2 14.6 %reshape.75 = bf16[8,128,4,4,256]{4,3,2,1,0:T(4,128)(2,1)} reshape(bf16[8,128,4096]{2,1,0:T(8,128)(2,1)} %param.24) | data formatting | bytes 16777216 | tf_op jit(solution)/shard_map/reshape | solution.py:141
  219.8 14.5 %reshape.76 = bf16[8,128,4,4,256]{4,3,2,1,0:T(4,128)(2,1)} reshape(bf16[8,128,4096]{2,1,0:T(8,128)(2,1)} %param.25) | data formatting | bytes 16777216 | tf_op jit(solution)/shard_map/reshape | solution.py:142
  234.4 4.0 reduce-scatter.24.cloned.1.call-done
  239.1 39.0 %reduce-scatter.16.cloned.1.call-done = bf16[32,2,1024]{2,0,1:T(8,128)(2,1)} async-done(((bf16[256,2,1024]{2,0,1:T(8,128)(2,1)}), bf16[32,2,1024]{2,0,1:T(8,128)(2,1)}) %reduce-scatter.16.cloned.1.call-update) | async-done | bytes 131088 | tf_op jit(solution)/shard_map/reduce_scatter | solution.py:26
  279.9 4.3 all-to-all-start.2
  284.3 4.7 all-to-all-done.2
  289.0 5.9 %fusion.7 = f32[8,4,4,2,128]{4,3,2,1,0:T(2,128)S(1)} fusion(bf16[8,128,4,4,256]{4,3,2,1,0:T(4,128)(2,1)} %reshape.75, bf16[4,8,2,4,256]{4,2,3,1,0:T(2,128)(2,1)S(1)} %all-to-all-done.2), kind=kOutput, calls=%fused_computation.10 | convolution fusion | flops 16777216 | bytes 8650752 | tf_op jit(solution)/shard_map/grshd,rlghd->rghsl/dot_general | solution.py:83
  297.7 7.4 %all_to_all.21 = bf16[4,8,2,4,256]{4,2,3,1,0:T(2,128)(2,1)S(1)} all-to-all(bf16[4,8,2,4,256]{4,2,3,1,0:T(2,128)(2,1)S(1)} %fusion.41), channel_id=1, replica_groups=mesh['gx'=8,'gy'=4] {'gy'}, dimensions={0} | all-to-all | bytes 262144 | tf_op jit(solution)/shard_map/all_to_all | solution.py:36
  306.0 24.7 %all-gather.5.cloned.1.call-done = bf16[256,2,1024]{2,0,1:T(8,128)(2,1)} async-done(((bf16[32,2,1024]{2,0,1:T(8,128)(2,1)}), bf16[256,2,1024]{2,0,1:T(8,128)(2,1)}) %all-gather.5.cloned.1.call-update) | async-done | bytes 1048592 | tf_op jit(solution)/shard_map/all_gather | solution.py:41
  330.6 2.7 convolution_convert_fusion.1
  333.4 20.5 %reduce-scatter.18.cloned.1.call-done = bf16[64,2,512]{2,0,1:T(8,128)(2,1)} async-done(((bf16[256,2,512]{2,0,1:T(8,128)(2,1)}), bf16[64,2,512]{2,0,1:T(8,128)(2,1)}) %reduce-scatter.18.cloned.1.call-update) | async-done | bytes 131088 | tf_op jit(solution)/shard_map/reduce_scatter | solution.py:49
  354.8 13.2 %all_gather.19 = bf16[256,2,512]{2,0,1:T(8,128)(2,1)S(1)} all-gather(bf16[64,2,512]{2,0,1:T(8,128)(2,1)S(1)} %add_convert_fusion.1), channel_id=1, replica_groups=mesh['gx'=8,'gy'=4] {'gy'}, dimensions={0}, use_global_device_ids=true | all-gather | bytes 655360 | tf_op jit(solution)/shard_map/all_gather | solution.py:15
  368.0 25.3 %fusion.9 = bf16[256,2,2,4096]{3,0,2,1:T(8,128)(2,1)} fusion(bf16[512,2,4096]{2,1,0:T(2,128)(2,1)} %param.20, bf16[256,2,512]{2,0,1:T(8,128)(2,1)S(1)} %all_gather.19, f32[512]{0:T(512)S(1)} %bitcast.90), kind=kOutput, calls=%fused_computation.12 | convolution fusion | flops 4299948032 | bytes 17303552 | tf_op jit(solution)/shard_map/dot_general | solution.py:18
  393.6 15.5 %psum.15 = bf16[256,2]{0,1:T(2,128)(2,1)S(1)} all-reduce(bf16[256,2]{0,1:T(2,128)(2,1)S(1)} %fusion.49), channel_id=1, replica_groups=mesh['gx'=8,'gy'=4] {'gx'}, use_global_device_ids=true, to_apply=%region_13.14 | all-reduce | flops 512 | bytes 2048 | tf_op jit(solution)/shard_map/psum | solution.py:151
  409.1 112.9 %all-reduce.2.cloned.1.call-done = bf16[256,2,2,4096]{3,0,2,1:T(8,128)(2,1)} async-done(((bf16[256,2,2,4096]{3,0,2,1:T(8,128)(2,1)}), bf16[256,2,2,4096]{3,0,2,1:T(8,128)(2,1)}) %all-reduce.2.cloned.1.call-update) | async-done | bytes 8388624 | tf_op jit(solution)/shard_map/psum | solution.py:150
  522.0 11.7 %convert_multiply_fusion = f32[256,2,2,4096]{3,0,2,1:T(8,128)} fusion(bf16[256,2,2,4096]{3,0,2,1:T(8,128)(2,1)} %all-reduce.2.cloned.1.call-done, f32[256,2]{0,1:T(2,128)S(1)} %add_rsqrt_fusion), kind=kLoop, calls=%fused_computation | loop fusion | flops 8388608 | bytes 25167872 | tf_op jit(solution)/shard_map/mul | solution.py:153
  533.7 10.3 %fusion.24 = bf16[256,2,512]{2,0,1:T(8,128)(2,1)} fusion(bf16[4096,512]{1,0:T(8,128)(2,1)} %param.21, f32[256,2,2,4096]{3,0,2,1:T(8,128)} %convert_multiply_fusion), kind=kOutput, calls=%fused_computation.31 | convolution fusion | flops 2160328704 | bytes 21495808 | tf_op jit(solution)/shard_map/dot_general | solution.py:155
  544.0 21.5 %reduce-scatter.20.cloned.1.call-done = bf16[64,2,512]{2,0,1:T(8,128)(2,1)} async-done(((bf16[256,2,512]{2,0,1:T(8,128)(2,1)}), bf16[64,2,512]{2,0,1:T(8,128)(2,1)}) %reduce-scatter.20.cloned.1.call-update) | async-done | bytes 131088 | tf_op jit(solution)/shard_map/reduce_scatter | solution.py:49
  (84 shorter events, 23.7 us)
Async XLA Ops:
  6.5 17.4 %copy-start = (bf16[512,3,1024]{2,0,1:T(8,128)(2,1)S(1)}, bf16[512,3,1024]{2,0,1:T(8,128)(2,1)}, u32[]{:S(2)}) copy-start(bf16[512,3,1024]{2,0,1:T(8,128)(2,1)} %param.16) | copy-start | bytes 9437188
  6.5 51.7 %reduce-scatter.22.cloned.1.call-start = ((), (), s32[]{:S(2)}) async-start(), calls=%async_computation.19 | async-start | bytes 73728
  21.3 0.8 copy-start.3
  23.1 85.6 %reduce-scatter.12.cloned.1.call-start = ((), (), s32[]{:S(2)}) async-start(), calls=%async_computation.11 | async-start | bytes 3538944 | tf_op jit(solution)/shard_map/reduce_scatter | solution.py:26
  28.5 91.4 %copy-start.4 = (bf16[8,32,4096]{2,1,0:T(8,128)(2,1)S(1)}, bf16[8,32,4096]{2,1,0:T(8,128)(2,1)}, u32[]{:S(2)}) copy-start(bf16[8,32,4096]{2,1,0:T(8,128)(2,1)} %param.23) | copy-start | bytes 6291460
  28.5 94.1 %copy-start.9 = (s32[8]{0:T(128)S(1)}, s32[8]{0:T(128)}, u32[]{:S(2)}) copy-start(s32[8]{0:T(128)} %param.26) | copy-start | bytes 100
  111.0 15.2 %all-to-all-start = ((bf16[4,8,2,3,4,256]{5,2,4,1,3,0:T(2,128)(2,1)}), bf16[4,8,2,3,4,256]{5,2,4,1,3,0:T(2,128)(2,1)S(1)}, u32[]{:S(2)}, u32[]{:S(2)}) async-start(bf16[4,8,2,3,4,256]{5,2,4,1,3,0:T(2,128)(2,1)} %copy.124), calls=%async_computation.1 | async-start | bytes 786432 | tf_op jit(solution)/shard_map/all_to_all | solution.py:36
  115.3 50.0 %all-gather.3.cloned.1.call-start = ((), (), s32[]{:S(2)}) async-start(), calls=%async_computation.12 | async-start | bytes 1179648 | tf_op jit(solution)/shard_map/all_gather | solution.py:41
  119.8 68.8 %copy-start.5 = (bf16[64,2,512]{2,1,0:T(2,128)(2,1)S(1)}, bf16[64,2,512]{2,1,0:T(2,128)(2,1)}, u32[]{:S(2)}) copy-start(bf16[64,2,512]{2,1,0:T(2,128)(2,1)} %param.14) | copy-start | bytes 393220
  122.6 42.8 %copy-start.6 = (bf16[1024,512]{1,0:T(8,128)(2,1)S(1)}, bf16[1024,512]{1,0:T(8,128)(2,1)}, u32[]{:S(2)}) copy-start(bf16[1024,512]{1,0:T(8,128)(2,1)} %param.17) | copy-start | bytes 3145732
  130.4 73.0 %copy-start.7 = (bf16[512,1024]{1,0:T(8,128)(2,1)S(1)}, bf16[512,1024]{1,0:T(8,128)(2,1)}, u32[]{:S(2)}) copy-start(bf16[512,1024]{1,0:T(8,128)(2,1)} %param.18) | copy-start | bytes 3145732
  140.8 47.8 %reduce-scatter.14.cloned.1.call-start = ((), (), s32[]{:S(2)}) async-start(), calls=%async_computation.13 | async-start | bytes 655360 | tf_op jit(solution)/shard_map/reduce_scatter | solution.py:49
  168.1 70.2 %reduce-scatter.24.cloned.1.call-start = ((), (), s32[]{:S(2)}) async-start(), calls=%async_computation.20 | async-start | bytes 73728
  203.4 74.7 %reduce-scatter.16.cloned.1.call-start = ((), (), s32[]{:S(2)}) async-start(), calls=%async_computation.14 | async-start | bytes 1179648 | tf_op jit(solution)/shard_map/reduce_scatter | solution.py:26
  219.8 64.4 %copy-start.10 = (s32[8]{0:T(128)S(1)}, s32[8]{0:T(128)}, u32[]{:S(2)}) copy-start(s32[8]{0:T(128)} %param.27) | copy-start | bytes 100
  279.9 9.1 %all-to-all-start.2 = ((bf16[4,8,2,4,256]{4,2,3,1,0:T(2,128)(2,1)}), bf16[4,8,2,4,256]{4,2,3,1,0:T(2,128)(2,1)S(1)}, u32[]{:S(2)}, u32[]{:S(2)}) async-start(bf16[4,8,2,4,256]{4,2,3,1,0:T(2,128)(2,1)} %copy.137), calls=%async_computation.5 | async-start | bytes 262144 | tf_op jit(solution)/shard_map/all_to_all | solution.py:36
  284.2 46.4 %all-gather.5.cloned.1.call-start = ((), (), s32[]{:S(2)}) async-start(), calls=%async_computation.15 | async-start | bytes 1179648 | tf_op jit(solution)/shard_map/all_gather | solution.py:41
  289.0 6.2 %copy-start.2 = (bf16[8,128,4,4,256]{4,3,2,1,0:T(4,128)(2,1)S(1)}, bf16[8,128,4,4,256]{4,3,2,1,0:T(4,128)(2,1)}, u32[]{:S(2)}) copy-start(bf16[8,128,4,4,256]{4,3,2,1,0:T(4,128)(2,1)} %reshape.76) | copy-start | bytes 25165828
  294.9 35.7 %copy-start.8 = (bf16[1024,512]{1,0:T(8,128)(2,1)S(1)}, bf16[1024,512]{1,0:T(8,128)(2,1)}, u32[]{:S(2)}) copy-start(bf16[1024,512]{1,0:T(8,128)(2,1)} %param.19) | copy-start | bytes 3145732
  305.9 48.0 %reduce-scatter.18.cloned.1.call-start = ((), (), s32[]{:S(2)}) async-start(), calls=%async_computation.16 | async-start | bytes 655360 | tf_op jit(solution)/shard_map/reduce_scatter | solution.py:49
  333.4 188.6 %all-reduce.2.cloned.1.call-start = ((), (), s32[]{:S(2)}) async-start(), calls=%async_computation.17 | async-start | bytes 16777216 | tf_op jit(solution)/shard_map/psum | solution.py:150
  393.4 172.1 %reduce-scatter.20.cloned.1.call-start = ((), (), s32[]{:S(2)}) async-start(), calls=%async_computation.18 | async-start | bytes 655360 | tf_op jit(solution)/shard_map/reduce_scatter | solution.py:49
  533.7 33.5 %copy-start.1 = (bf16[512,3,1024]{2,0,1:T(8,128)(2,1)S(1)}, bf16[512,3,1024]{2,0,1:T(8,128)(2,1)}, u32[]{:S(2)}) copy-start(bf16[512,3,1024]{2,0,1:T(8,128)(2,1)} %param.16) | copy-start | bytes 9437188
Sparse Core Ops, SparseCore 0:
  23.2 34.9 reduce-scatter.21
  62.0 46.7 reduce-scatter.11
  140.9 24.3 all-gather.2
  168.2 20.3 reduce-scatter.13
  203.5 34.7 reduce-scatter.23
  241.7 36.3 reduce-scatter.15
  306.0 24.5 all-gather.4
  333.5 20.3 reduce-scatter.17
  393.5 128.4 all-reduce.1
  544.1 21.3 reduce-scatter.19
where the time goes:
time: 579 us; the launch traced here: 574 us
  waiting for transfers between devices  355 us (61%)
  blocking collectives  70.9 us (12%)
  matrix products  60.9 us (11%)
  local copies, waits for them, and re-layouts  46.2 us (8%)
  other arithmetic  18.2 us (3%)
  between operations  13.7 us (2%)
  starting transfers between devices  8.93 us (2%)
    psum x1, waiting for transfers between devices, per_device(): lax.psum(ffn_partials[0].astype(jnp.bfloat16), 'gx').astype(jnp.float32)  113 us
    reduce_scatter x2, waiting for transfers between devices, combine_rows(): lax.psum_scatter(partials[0].astype(jnp.bfloat16), 'gx', scatter_dimensio...  88.7 us
    reduce_scatter x3, waiting for transfers between devices, sum_out(): lax.psum_scatter(partials.astype(jnp.bfloat16), 'gy', scatter_dimension=0...  62.4 us
    all_gather x2, waiting for transfers between devices, project_out(): lax.all_gather(activity, 'gx', axis=0, tiled=True)  49.1 us
    all_gather x3, blocking collectives, gather_in(): lax.all_gather(stream, 'gy', axis=0, tiled=True).astype(jnp.float32)  40.8 us
    unnamed x12, waiting for transfers between devices  33.8 us
    dot_general x3, matrix products, gather_in(): lax.dot_general(scaled, weight, (((2,), (0,)), ((), ())), preferred_eleme...  31.5 us
    psum x1, blocking collectives, per_device(): lax.psum(ffn_partials[1].astype(jnp.bfloat16), 'gx').astype(jnp.float32)  15.5 us
  transfers between devices with their start and end apart: 12, of which 12 were waited for; matrix products, arithmetic and copies ran while one was open for 8% of the time, Pallas kernels for 0%

commit v1 on v0

v1 whole, which is shorter than its diff:
```python
import functools

import jax
import jax.numpy as jnp
from jax import lax
from jax.experimental import pallas as pl
from jax.experimental.pallas import tpu as pltpu
from jax.sharding import PartitionSpec as P

D = 4096
HEAD_DIM = 256
NEW = 2
EPSILON = 1e-06
LANES = 128
MESH = pl.DeviceIdType.MESH
VMEM_LIMIT = 58 * 1024 * 1024


def remote(src, dst, send, recv, device):
    return pltpu.make_async_remote_copy(
        src_ref=src,
        dst_ref=dst,
        send_sem=send,
        recv_sem=recv,
        device_id=device,
        device_id_type=MESH,
    )


def entry_barrier(n, m, i, g):
    barrier = pltpu.get_barrier_semaphore()
    for k in range(1, n):
        pl.semaphore_signal(
            barrier, inc=1, device_id=(lax.rem(i + k, n), g), device_id_type=MESH
        )
    for k in range(1, m):
        pl.semaphore_signal(
            barrier, inc=1, device_id=(i, lax.rem(g + k, m)), device_id_type=MESH
        )
    pl.semaphore_wait(barrier, n + m - 2)


def rows_at(start, size):
    return pl.ds(pl.multiple_of(start * size, size), size)


def project_kernel(
    n, m, blocks, silu,
    x_ref, gain_ref, w_ref, out_ref,
    xg, scaled, part, landed, mine, arrived, total,
    gs, gr, ps, pr, cs, cr, as_, ar,
):
    i, g = lax.axis_index("gx"), lax.axis_index("gy")
    half = n // 2
    c, q = lax.rem(i, 2), i // 2
    other = 1 - c
    partner = q * 2 + other
    here = x_ref.shape[0]
    rows = xg.shape[0] // n
    entry_barrier(n, m, i, g)

    sends = []
    for k in range(1, m):
        copy = remote(
            x_ref, xg.at[rows_at(g, here)], gs.at[k - 1], gr.at[k - 1],
            (i, lax.rem(g + k, m)),
        )
        copy.start()
        sends.append(copy)
    xg[rows_at(g, here), :] = x_ref[...]
    for copy in sends:
        copy.wait_recv()

    gain = gain_ref[...]
    squares = []
    for side in range(2):
        parity = other if side == 0 else c
        sums = []
        for chunk in range(half):
            wide = xg[rows_at(2 * chunk + parity, rows), :].astype(jnp.float32)
            sums.append(jnp.sum(wide * wide, axis=1, keepdims=True))
            scaled[side, pl.ds(chunk * rows, rows), :] = (wide * gain).astype(jnp.bfloat16)
        squares.append(jnp.concatenate(sums, axis=0))

    def block_product(side, block):
        j, start, width, _ = block
        if j < 0:
            return jnp.broadcast_to(squares[side], (half * rows, width))
        return jnp.dot(
            scaled[side], w_ref[j, :, pl.ds(start, width)],
            preferred_element_type=jnp.float32,
        )

    pair = []
    for b, block in enumerate(blocks):
        _, _, width, at = block
        columns = pl.ds(at, width)
        part[:, columns] = block_product(0, block).astype(jnp.bfloat16)
        copy = remote(
            part.at[:, columns], landed.at[:, columns], ps.at[b], pr.at[b], (partner, g)
        )
        copy.start()
        pair.append(copy)

    cross = []
    for b, block in enumerate(blocks):
        _, _, width, at = block
        columns = pl.ds(at, width)
        product = block_product(1, block)
        pair[b].wait_recv()
        mine[:, columns] = (product + landed[:, columns].astype(jnp.float32)).astype(
            jnp.bfloat16
        )
        for k in range(1, half):
            target = lax.rem(q + k, half)
            copy = remote(
                mine.at[rows_at(target, rows), columns], arrived.at[k - 1, :, columns],
                cs.at[k - 1, b], cr.at[k - 1, b], (target * 2 + c, g),
            )
            copy.start()
            cross.append((b, k, copy))

    for b, block in enumerate(blocks):
        _, _, width, at = block
        columns = pl.ds(at, width)
        for bb, k, copy in cross:
            if bb == b:
                copy.wait_recv()
        summed = mine[rows_at(q, rows), columns].astype(jnp.float32)
        for k in range(1, half):
            summed = summed + arrived[k - 1, :, columns].astype(jnp.float32)
        total[:, columns] = summed

    n_columns = blocks[-1][3]
    factor = lax.rsqrt(total[:, pl.ds(n_columns, 1)] / D + EPSILON)
    if silu:
        width = n_columns // 2
        step = min(width, 1024)
        for at in range(0, width, step):
            gate = total[:, pl.ds(at, step)] * factor
            up = total[:, pl.ds(width + at, step)] * factor
            out_ref[:, pl.ds(at, step)] = (
                gate / (1.0 + jnp.exp(-gate)) * up
            ).astype(jnp.bfloat16)
    else:
        piece = rows // m
        scaled_out = mine.at[rows_at(q, rows), pl.ds(0, n_columns)]
        scaled_out[...] = (total[:, pl.ds(0, n_columns)] * factor).astype(jnp.bfloat16)
        away = []
        for k in range(1, m):
            target = lax.rem(g + k, m)
            copy = remote(
                mine.at[
                    pl.ds(pl.multiple_of(q * rows + target * piece, piece), piece),
                    pl.ds(0, n_columns),
                ],
                out_ref.at[g], as_.at[k - 1], ar.at[k - 1], (i, target),
            )
            copy.start()
            away.append(copy)
        out_ref[g] = mine[
            pl.ds(pl.multiple_of(q * rows + g * piece, piece), piece), pl.ds(0, n_columns)
        ]
        for copy in away:
            copy.wait()

    for copy in sends + pair:
        copy.wait_send()
    for _, _, copy in cross:
        copy.wait_send()


def project(n, m, collective_id, silu, x, gain, weight):
    parts, features, width = weight.shape
    here = x.shape[0]
    tokens = here * m
    rows = tokens // n
    half = n // 2
    step = width
    while step > 1024 and step % 2 == 0:
        step //= 2
    if parts == 1 and step == width and width % 512 == 0:
        step = width // 2
    blocks = [
        (j, at, step, j * width + at) for j in range(parts) for at in range(0, width, step)
    ]
    columns = parts * width
    blocks.append((-1, 0, LANES, columns))
    held = columns + LANES
    count = len(blocks)
    if silu:
        out = jax.ShapeDtypeStruct((rows, width), jnp.bfloat16)
    else:
        out = jax.ShapeDtypeStruct((m, rows // m, columns), jnp.bfloat16)
    dma = pltpu.SemaphoreType.DMA
    return pl.pallas_call(
        functools.partial(project_kernel, n, m, tuple(blocks), silu),
        out_shape=out,
        in_specs=[pl.BlockSpec(memory_space=pltpu.VMEM)] * 3,
        out_specs=pl.BlockSpec(memory_space=pltpu.VMEM),
        scratch_shapes=[
            pltpu.VMEM((tokens, features), jnp.bfloat16),
            pltpu.VMEM((2, half * rows, features), jnp.bfloat16),
            pltpu.VMEM((half * rows, held), jnp.bfloat16),
            pltpu.VMEM((half * rows, held), jnp.bfloat16),
            pltpu.VMEM((half * rows, held), jnp.bfloat16),
            pltpu.VMEM((half - 1, rows, held), jnp.bfloat16),
            pltpu.VMEM((rows, held), jnp.float32),
            dma((m - 1,)), dma((m - 1,)),
            dma((count,)), dma((count,)),
            dma((half - 1, count)), dma((half - 1, count)),
            dma((m - 1,)), dma((m - 1,)),
        ],
        compiler_params=pltpu.CompilerParams(
            collective_id=collective_id, has_side_effects=True, vmem_limit_bytes=VMEM_LIMIT
        ),
    )(x, gain, weight)


def output_kernel(
    n, m, regroup,
    a_ref, w_ref, res_ref, out_ref,
    act, part, landed,
    as_, ar, cs, cr, ps, pr, gs, gr,
):
    i, g = lax.axis_index("gx"), lax.axis_index("gy")
    half = n // 2
    c, q = lax.rem(i, 2), i // 2
    partner = q * 2 + 1 - c
    here = res_ref.shape[0]
    rows = act.shape[1]
    entry_barrier(n, m, i, g)

    sends = []
    if regroup:
        piece = rows // m
        away = []
        for k in range(1, m):
            target = lax.rem(g + k, m)
            copy = remote(
                a_ref.at[target], act.at[i, rows_at(g, piece)],
                as_.at[k - 1], ar.at[k - 1], (i, target),
            )
            copy.start()
            away.append(copy)
        act[i, rows_at(g, piece), :] = a_ref[g]
        for copy in away:
            copy.wait_recv()
        sends += away
    else:
        act[i] = a_ref[...]

    cross = []
    for k in range(1, half):
        copy = remote(
            act.at[i], act.at[i], cs.at[k - 1], cr.at[k - 1],
            (lax.rem(q + k, half) * 2 + c, g),
        )
        copy.start()
        cross.append(copy)
    pair = []
    for k in range(half):
        chip = lax.rem(q + half - k, half)
        source = chip * 2 + c
        if k > 0:
            cross[k - 1].wait_recv()
        copy = remote(act.at[source], act.at[source], ps.at[k], pr.at[k], (partner, g))
        copy.start()
        pair.append(copy)
        if k > 0:
            multiply(act, w_ref, part, pair[k - 1], lax.rem(q + half - (k - 1), half), rows)
    multiply(act, w_ref, part, pair[half - 1], lax.rem(q + 1, half), rows)

    summed = []
    for k in range(1, m):
        target = lax.rem(g + k, m)
        copy = remote(
            part.at[rows_at(target, here)], landed.at[k - 1],
            gs.at[k - 1], gr.at[k - 1], (i, target),
        )
        copy.start()
        summed.append(copy)
    result = part[rows_at(g, here), :].astype(jnp.float32)
    for k in range(1, m):
        summed[k - 1].wait_recv()
        result = result + landed[k - 1].astype(jnp.float32)
    out_ref[...] = (res_ref[...].astype(jnp.float32) + result).astype(jnp.bfloat16)
    for copy in sends + cross + pair + summed:
        copy.wait_send()


def multiply(act, w_ref, part, copy, chip, rows):
    copy.wait_recv()
    block = act[pl.ds(chip * 2, 2)].reshape(2 * rows, act.shape[2])
    part[rows_at(chip, 2 * rows), :] = jnp.dot(
        block, w_ref[...], preferred_element_type=jnp.float32
    ).astype(jnp.bfloat16)


def output(n, m, collective_id, regroup, activity, weight, residual):
    here, features = residual.shape
    tokens = here * m
    rows = tokens // n
    half = n // 2
    dma = pltpu.SemaphoreType.DMA
    return pl.pallas_call(
        functools.partial(output_kernel, n, m, regroup),
        out_shape=jax.ShapeDtypeStruct((here, features), jnp.bfloat16),
        in_specs=[pl.BlockSpec(memory_space=pltpu.VMEM)] * 3,
        out_specs=pl.BlockSpec(memory_space=pltpu.VMEM),
        scratch_shapes=[
            pltpu.VMEM((n, rows, weight.shape[0]), jnp.bfloat16),
            pltpu.VMEM((tokens, features), jnp.bfloat16),
            pltpu.VMEM((m - 1, here, features), jnp.bfloat16),
            dma((m - 1,)), dma((m - 1,)),
            dma((half - 1,)), dma((half - 1,)),
            dma((half,)), dma((half,)),
            dma((m - 1,)), dma((m - 1,)),
        ],
        compiler_params=pltpu.CompilerParams(
            collective_id=collective_id, has_side_effects=True, vmem_limit_bytes=VMEM_LIMIT
        ),
    )(activity, weight, residual)


def contract(left, right):
    return lax.dot_general(
        left, right, (((1,), (1,)), ((), ())), preferred_element_type=jnp.float32
    )


def attend_kernel(heads, own, q_ref, k_ref, v_ref, length_ref, out_ref):
    rows, slots, _ = k_ref.shape
    count = q_ref.shape[1]
    scale = HEAD_DIM ** (-0.5)
    shape = (count, rows * slots)
    row = lax.broadcasted_iota(jnp.int32, shape, 0) // NEW
    column = lax.broadcasted_iota(jnp.int32, shape, 1)
    slot = column - row * slots
    visible = (slot >= 0) & (slot < length_ref[...])
    if own:
        mine = (count, count)
        token = lax.broadcasted_iota(jnp.int32, mine, 0)
        key = lax.broadcasted_iota(jnp.int32, mine, 1)
        causal = (token // NEW == key // NEW) & (key <= token)
    for h in range(heads):
        span = pl.ds(h * HEAD_DIM, HEAD_DIM)
        query = q_ref[0, :, span]
        keys = k_ref[:, :, span].reshape(rows * slots, HEAD_DIM)
        values = v_ref[:, :, span].reshape(rows * slots, HEAD_DIM)
        exps = jnp.where(visible, jnp.exp(contract(query, keys) * scale), 0.0)
        totals = jnp.sum(exps, axis=1, keepdims=True)
        if own:
            new_keys = q_ref[0, :, pl.ds((heads + h) * HEAD_DIM, HEAD_DIM)]
            new_values = q_ref[0, :, pl.ds((2 * heads + h) * HEAD_DIM, HEAD_DIM)]
            fresh = jnp.where(causal, jnp.exp(contract(query, new_keys) * scale), 0.0)
            totals = totals + jnp.sum(fresh, axis=1, keepdims=True)
        mix = jnp.dot(
            (exps / totals).astype(jnp.bfloat16), values, preferred_element_type=jnp.float32
        )
        if own:
            mix = mix + jnp.dot(
                (fresh / totals).astype(jnp.bfloat16), new_values,
                preferred_element_type=jnp.float32,
            )
        out_ref[0, :, span] = mix.astype(jnp.bfloat16)


def attend(own, queries, keys, values, lengths):
    m, count, columns = queries.shape
    rows, slots, features = keys.shape
    width = features // m
    spread = jnp.repeat(lengths, count // rows).reshape(count, 1)
    return pl.pallas_call(
        functools.partial(attend_kernel, width // HEAD_DIM, own),
        out_shape=jax.ShapeDtypeStruct((m, count, width), jnp.bfloat16),
        grid=(m,),
        in_specs=[
            pl.BlockSpec((1, count, columns), lambda s: (s, 0, 0)),
            pl.BlockSpec((rows, slots, width), lambda s: (0, 0, s)),
            pl.BlockSpec((rows, slots, width), lambda s: (0, 0, s)),
            pl.BlockSpec((count, 1), lambda s: (0, 0)),
        ],
        out_specs=pl.BlockSpec((1, count, width), lambda s: (s, 0, 0)),
        compiler_params=pltpu.CompilerParams(vmem_limit_bytes=VMEM_LIMIT),
    )(queries, keys, values, spread)


def per_device(
    tokens,
    gains,
    w_qkv,
    w_self_out,
    w_cross_q,
    w_cross_out,
    w_ffn_in,
    w_ffn_out,
    self_keys,
    self_values,
    cross_keys,
    cross_values,
    positions,
    src_len,
):
    n, m = lax.axis_size("gx"), lax.axis_size("gy")
    stream = tokens.reshape(tokens.shape[0] * NEW, tokens.shape[2])
    projected = project(n, m, 0, False, stream, gains[0:1], jnp.transpose(w_qkv, (1, 0, 2)))
    mixed = attend(True, projected, self_keys, self_values, positions)
    after_self = output(n, m, 1, True, mixed, w_self_out, stream)
    queries = project(n, m, 2, False, after_self, gains[1:2], w_cross_q[None])
    crossed = attend(False, queries, cross_keys, cross_values, src_len)
    after_cross = output(n, m, 3, True, crossed, w_cross_out, after_self)
    hidden = project(
        n, m, 4, True, after_cross, gains[2:3], jnp.transpose(w_ffn_in, (1, 0, 2))
    )
    result = output(n, m, 5, False, hidden, w_ffn_out, after_cross)
    return result.reshape(tokens.shape)


def solution(mesh):
    return jax.shard_map(
        per_device,
        mesh=mesh,
        in_specs=(
            P("gy", None, "gx"),
            P(None, "gx"),
            P("gx", None, "gy"),
            P("gy", "gx"),
            P("gx", "gy"),
            P("gy", "gx"),
            P("gx", None, "gy"),
            P("gy", "gx"),
            P(("gx", "gy"), None, None),
            P(("gx", "gy"), None, None),
            P(("gx", "gy"), None, None),
            P(("gx", "gy"), None, None),
            P(("gx", "gy")),
            P(("gx", "gy")),
        ),
        out_specs=P("gy", None, "gx"),
        check_vma=False,
    )
```

time: 579 us -> 300 us (0.52)
  waiting for transfers between devices: 355 us -> 0 us
  Pallas kernels: 0 us -> 276 us
  blocking collectives: 70.9 us -> 0 us
  matrix products: 60.9 us -> 0 us
  local copies, waits for them, and re-layouts: 46.2 us -> 20.1 us
  other arithmetic: 18.2 us -> 0 us
  between operations: 13.7 us -> 0.05 us
  starting transfers between devices: 8.93 us -> 0 us
    pallas_call x0 -> x8, Pallas kernels: none -> 276 us  [the longest x3 152 us: project(): pl.pallas_call(functools.partial(project_kernel, n, m, tuple(blocks), sil...]
    reduce_scatter x5 -> x0, waiting for transfers between devices: 151 us -> none  [the longest x2 88.7 us: combine_rows(): lax.psum_scatter(partials[0].astype(jnp.bfloat16), 'gx', scatter_dimensio...]
    psum x1 -> x0, waiting for transfers between devices: 113 us -> none  [per_device(): lax.psum(ffn_partials[0].astype(jnp.bfloat16), 'gx').astype(jnp.float32)]
    dot_general x12 -> x0, matrix products: 60.9 us -> none  [the longest x3 31.5 us: gather_in(): lax.dot_general(scaled, weight, (((2,), (0,)), ((), ())), preferred_eleme...]
    all_gather x2 -> x0, waiting for transfers between devices: 49.1 us -> none  [project_out(): lax.all_gather(activity, 'gx', axis=0, tiled=True)]
    all_gather x3 -> x0, blocking collectives: 40.8 us -> none  [gather_in(): lax.all_gather(stream, 'gy', axis=0, tiled=True).astype(jnp.float32)]
    reshape x8 -> x2, local copies, waits for them, and re-layouts: 39.8 us -> 3.23 us  [the longest x1 1.62 us: per_device(): return result.reshape(tokens.shape)]
    unnamed x12 -> x0, waiting for transfers between devices: 33.8 us -> none
  transfers between devices with their start and end apart: 12 -> 0, of which waited for: 12 -> 0; matrix products, arithmetic and copies ran while one was open for 8% -> 0% of each run, Pallas kernels for 0% -> 0%
where the time goes in v1:
time: 300 us; the launch traced here: 297 us
  Pallas kernels  276 us (92%)
  local copies, waits for them, and re-layouts  20.1 us (7%)
    pallas_call x3, Pallas kernels, project(): pl.pallas_call(functools.partial(project_kernel, n, m, tuple(blocks), sil...  152 us
    pallas_call x3, Pallas kernels, output(): pl.pallas_call(functools.partial(output_kernel, n, m, regroup), out_shape...  106 us
    pallas_call x2, Pallas kernels, attend(): pl.pallas_call(functools.partial(attend_kernel, width // HEAD_DIM, own),...  18.3 us
    unnamed x1, local copies, waits for them, and re-layouts  12.6 us

profile of v1, /device:TPU:7, one launch (start us, length us, event | category | flops | bytes accessed | tf_op | source)
XLA Modules:
  0.0 296.5 jit_solution(14416119559612550416)
XLA Ops:
  0.0 0.7 broadcast_in_dim.9
  0.7 0.7 reshape_reshape.8.length_ref
  1.4 0.7 broadcast_in_dim.11
  2.1 0.7 reshape_reshape.9.length_ref
  2.8 1.4 fusion
  4.2 1.6 reshape.6.x_ref.res_ref
  5.8 48.1 %shard_map.136.q_ref = bf16[4,16,3072]{2,1,0:T(8,128)(2,1)} custom-call(bf16[128,512]{1,0:T(8,128)(2,1)} %reshape.6.x_ref.res_ref, f32[1,512]{1,0:T(1,128)} %get-tuple-element.6.gain_ref, bf16[3,512,1024]{2,1,0:T(8,128)(2,1)} %bitcast.6), custom_call_target="tpu_custom_call" | custom-call | tf_op jit(solution)/shard_map/pallas_call | solution.py:196
  53.9 7.4 %shard_map.137.a_ref = bf16[4,16,1024]{2,1,0:T(8,128)(2,1)} custom-call(bf16[4,16,3072]{2,1,0:T(8,128)(2,1)} %shard_map.136.q_ref, bf16[8,32,4096]{2,1,0:T(8,128)(2,1)} %k_ref.2, bf16[8,32,4096]{2,1,0:T(8,128)(2,1)} %v_ref.2, s32[16,1]{1,0:T(8,128)} %reshape_reshape.8.length_ref), custom_call_target="tpu_custom_call" | custom-call | tf_op jit(solution)/shard_map/pallas_call | solution.py:374
  61.3 31.7 %shard_map.138.x_ref.res_ref = bf16[128,512]{1,0:T(8,128)(2,1)} custom-call(bf16[4,16,1024]{2,1,0:T(8,128)(2,1)} %shard_map.137.a_ref, bf16[1024,512]{1,0:T(8,128)(2,1)} %w_ref.3, bf16[128,512]{1,0:T(8,128)(2,1)} %reshape.6.x_ref.res_ref), custom_call_target="tpu_custom_call" | custom-call | tf_op jit(solution)/shard_map/pallas_call | solution.py:306
  93.0 33.1 %shard_map.139.q_ref = bf16[4,16,1024]{2,1,0:T(8,128)(2,1)} custom-call(bf16[128,512]{1,0:T(8,128)(2,1)} %shard_map.138.x_ref.res_ref, f32[1,512]{1,0:T(1,128)} %get-tuple-element.7.gain_ref, bf16[1,512,1024]{2,1,0:T(8,128)(2,1)} %bitcast.7), custom_call_target="tpu_custom_call" | custom-call | tf_op jit(solution)/shard_map/pallas_call | solution.py:196
  126.2 11.0 %shard_map.140.a_ref = bf16[4,16,1024]{2,1,0:T(8,128)(2,1)} custom-call(bf16[4,16,1024]{2,1,0:T(8,128)(2,1)} %shard_map.139.q_ref, bf16[8,128,4096]{2,1,0:T(8,128)(2,1)} %k_ref.3, bf16[8,128,4096]{2,1,0:T(8,128)(2,1)} %v_ref.3, s32[16,1]{1,0:T(8,128)} %reshape_reshape.9.length_ref), custom_call_target="tpu_custom_call" | custom-call | tf_op jit(solution)/shard_map/pallas_call | solution.py:374
  137.1 28.0 %shard_map.141.x_ref.res_ref = bf16[128,512]{1,0:T(8,128)(2,1)} custom-call(bf16[4,16,1024]{2,1,0:T(8,128)(2,1)} %shard_map.140.a_ref, bf16[1024,512]{1,0:T(8,128)(2,1)} %w_ref.4, bf16[128,512]{1,0:T(8,128)(2,1)} %shard_map.138.x_ref.res_ref), custom_call_target="tpu_custom_call" | custom-call | tf_op jit(solution)/shard_map/pallas_call | solution.py:306
  165.1 12.6 %copy.22 = bf16[512,2,4096]{2,0,1:T(8,128)(2,1)} copy(bf16[512,2,4096]{2,1,0:T(2,128)(2,1)} %param.20) | data formatting | bytes 16777216 | tf_op args[6]
  177.8 71.1 %shard_map.142.a_ref = bf16[64,4096]{1,0:T(8,128)(2,1)} custom-call(bf16[128,512]{1,0:T(8,128)(2,1)} %shard_map.141.x_ref.res_ref, f32[1,512]{1,0:T(1,128)} %get-tuple-element.5.gain_ref, bf16[2,512,4096]{2,1,0:T(8,128)(2,1)} %bitcast.5), custom_call_target="tpu_custom_call" | custom-call | tf_op jit(solution)/shard_map/pallas_call | solution.py:196
  248.9 46.0 %shard_map.143 = bf16[128,512]{1,0:T(8,128)(2,1)} custom-call(bf16[64,4096]{1,0:T(8,128)(2,1)} %shard_map.142.a_ref, bf16[4096,512]{1,0:T(8,128)(2,1)} %w_ref.5, bf16[128,512]{1,0:T(8,128)(2,1)} %shard_map.141.x_ref.res_ref), custom_call_target="tpu_custom_call" | custom-call | tf_op jit(solution)/shard_map/pallas_call | solution.py:306
  294.9 1.6 reshape.7

commit v2 on v1

--- a/solution.py
+++ b/solution.py
@@ -48,7 +48,7 @@
     n, m, blocks, silu,
     x_ref, gain_ref, w_ref, out_ref,
     xg, scaled, part, landed, mine, arrived, total,
-    gs, gr, ps, pr, cs, cr, as_, ar,
+    held_w, gs, gr, ps, pr, cs, cr, as_, ar, ws,
 ):
     i, g = lax.axis_index("gx"), lax.axis_index("gy")
     half = n // 2
@@ -57,6 +57,12 @@
     partner = q * 2 + other
     here = x_ref.shape[0]
     rows = xg.shape[0] // n
+    loads = [
+        pltpu.make_async_copy(w_ref.at[j], held_w.at[j], ws.at[j])
+        for j in range(w_ref.shape[0])
+    ]
+    for load in loads:
+        load.start()
     entry_barrier(n, m, i, g)
 
     sends = []
@@ -87,10 +93,12 @@
         if j < 0:
             return jnp.broadcast_to(squares[side], (half * rows, width))
         return jnp.dot(
-            scaled[side], w_ref[j, :, pl.ds(start, width)],
+            scaled[side], held_w[j, :, pl.ds(start, width)],
             preferred_element_type=jnp.float32,
         )
 
+    for load in loads:
+        load.wait()
     pair = []
     for b, block in enumerate(blocks):
         _, _, width, at = block
@@ -120,6 +128,9 @@
             copy.start()
             cross.append((b, k, copy))
 
+    n_columns = blocks[0][3]
+    piece = rows // m
+    away = []
     for b, block in enumerate(blocks):
         _, _, width, at = block
         columns = pl.ds(at, width)
@@ -129,40 +140,38 @@
         summed = mine[rows_at(q, rows), columns].astype(jnp.float32)
         for k in range(1, half):
             summed = summed + arrived[k - 1, :, columns].astype(jnp.float32)
-        total[:, columns] = summed
-
-    n_columns = blocks[-1][3]
-    factor = lax.rsqrt(total[:, pl.ds(n_columns, 1)] / D + EPSILON)
+        if b == 0:
+            factor = lax.rsqrt(summed[:, 0:1] / D + EPSILON)
+        elif silu:
+            total[:, columns] = summed * factor
+        else:
+            mine[rows_at(q, rows), columns] = (summed * factor).astype(jnp.bfloat16)
+            for k in range(1, m):
+                target = lax.rem(g + k, m)
+                copy = remote(
+                    mine.at[
+                        pl.ds(pl.multiple_of(q * rows + target * piece, piece), piece),
+                        columns,
+                    ],
+                    out_ref.at[g, :, columns], as_.at[k - 1, b], ar.at[k - 1, b],
+                    (i, target),
+                )
+                copy.start()
+                away.append(copy)
+            out_ref[g, :, columns] = mine[
+                pl.ds(pl.multiple_of(q * rows + g * piece, piece), piece), columns
+            ]
     if silu:
         width = n_columns // 2
         step = min(width, 1024)
         for at in range(0, width, step):
-            gate = total[:, pl.ds(at, step)] * factor
-            up = total[:, pl.ds(width + at, step)] * factor
+            gate = total[:, pl.ds(at, step)]
+            up = total[:, pl.ds(width + at, step)]
             out_ref[:, pl.ds(at, step)] = (
                 gate / (1.0 + jnp.exp(-gate)) * up
             ).astype(jnp.bfloat16)
-    else:
-        piece = rows // m
-        scaled_out = mine.at[rows_at(q, rows), pl.ds(0, n_columns)]
-        scaled_out[...] = (total[:, pl.ds(0, n_columns)] * factor).astype(jnp.bfloat16)
-        away = []
-        for k in range(1, m):
-            target = lax.rem(g + k, m)
-            copy = remote(
-                mine.at[
-                    pl.ds(pl.multiple_of(q * rows + target * piece, piece), piece),
-                    pl.ds(0, n_columns),
-                ],
-                out_ref.at[g], as_.at[k - 1], ar.at[k - 1], (i, target),
-            )
-            copy.start()
-            away.append(copy)
-        out_ref[g] = mine[
-            pl.ds(pl.multiple_of(q * rows + g * piece, piece), piece), pl.ds(0, n_columns)
-        ]
-        for copy in away:
-            copy.wait()
+    for copy in away:
+        copy.wait()
 
     for copy in sends + pair:
         copy.wait_send()
@@ -185,7 +194,7 @@
         (j, at, step, j * width + at) for j in range(parts) for at in range(0, width, step)
     ]
     columns = parts * width
-    blocks.append((-1, 0, LANES, columns))
+    blocks.insert(0, (-1, 0, LANES, columns))
     held = columns + LANES
     count = len(blocks)
     if silu:
@@ -196,7 +205,11 @@
     return pl.pallas_call(
         functools.partial(project_kernel, n, m, tuple(blocks), silu),
         out_shape=out,
-        in_specs=[pl.BlockSpec(memory_space=pltpu.VMEM)] * 3,
+        in_specs=[
+            pl.BlockSpec(memory_space=pltpu.VMEM),
+            pl.BlockSpec(memory_space=pltpu.VMEM),
+            pl.BlockSpec(memory_space=pl.ANY),
+        ],
         out_specs=pl.BlockSpec(memory_space=pltpu.VMEM),
         scratch_shapes=[
             pltpu.VMEM((tokens, features), jnp.bfloat16),
@@ -206,10 +219,12 @@
             pltpu.VMEM((half * rows, held), jnp.bfloat16),
             pltpu.VMEM((half - 1, rows, held), jnp.bfloat16),
             pltpu.VMEM((rows, held), jnp.float32),
+            pltpu.VMEM(weight.shape, jnp.bfloat16),
             dma((m - 1,)), dma((m - 1,)),
             dma((count,)), dma((count,)),
             dma((half - 1, count)), dma((half - 1, count)),
-            dma((m - 1,)), dma((m - 1,)),
+            dma((m - 1, count)), dma((m - 1, count)),
+            dma((parts,)),
         ],
         compiler_params=pltpu.CompilerParams(
             collective_id=collective_id, has_side_effects=True, vmem_limit_bytes=VMEM_LIMIT
@@ -220,8 +235,8 @@
 def output_kernel(
     n, m, regroup,
     a_ref, w_ref, res_ref, out_ref,
-    act, part, landed,
-    as_, ar, cs, cr, ps, pr, gs, gr,
+    act, part, landed, held_w,
+    as_, ar, cs, cr, ps, pr, gs, gr, ws,
 ):
     i, g = lax.axis_index("gx"), lax.axis_index("gy")
     half = n // 2
@@ -229,6 +244,8 @@
     partner = q * 2 + 1 - c
     here = res_ref.shape[0]
     rows = act.shape[1]
+    load = pltpu.make_async_copy(w_ref, held_w, ws.at[0])
+    load.start()
     entry_barrier(n, m, i, g)
 
     sends = []
@@ -258,6 +275,30 @@
         )
         copy.start()
         cross.append(copy)
+    early = half == m and 2 * rows == here
+    summed = []
+    for k in range(1, m):
+        target = lax.rem(g + k, m)
+        summed.append(
+            remote(
+                part.at[rows_at(target, here)], landed.at[k - 1],
+                gs.at[k - 1], gr.at[k - 1], (i, target),
+            )
+        )
+
+    def finish(k):
+        chip = lax.rem(q + half - k, half)
+        multiply(act, held_w, part, pair[k], chip, rows)
+        if early:
+            ahead = lax.rem(chip + m - g, m)
+
+            @pl.when(ahead != 0)
+            def _():
+                remote(
+                    part.at[rows_at(chip, here)], landed.at[ahead - 1],
+                    gs.at[ahead - 1], gr.at[ahead - 1], (i, chip),
+                ).start()
+
     pair = []
     for k in range(half):
         chip = lax.rem(q + half - k, half)
@@ -267,19 +308,14 @@
         copy = remote(act.at[source], act.at[source], ps.at[k], pr.at[k], (partner, g))
         copy.start()
         pair.append(copy)
-        if k > 0:
-            multiply(act, w_ref, part, pair[k - 1], lax.rem(q + half - (k - 1), half), rows)
-    multiply(act, w_ref, part, pair[half - 1], lax.rem(q + 1, half), rows)
-
-    summed = []
-    for k in range(1, m):
-        target = lax.rem(g + k, m)
-        copy = remote(
-            part.at[rows_at(target, here)], landed.at[k - 1],
-            gs.at[k - 1], gr.at[k - 1], (i, target),
-        )
-        copy.start()
-        summed.append(copy)
+        if k == 0:
+            load.wait()
+        else:
+            finish(k - 1)
+    finish(half - 1)
+    if not early:
+        for copy in summed:
+            copy.start()
     result = part[rows_at(g, here), :].astype(jnp.float32)
     for k in range(1, m):
         summed[k - 1].wait_recv()
@@ -306,16 +342,22 @@
     return pl.pallas_call(
         functools.partial(output_kernel, n, m, regroup),
         out_shape=jax.ShapeDtypeStruct((here, features), jnp.bfloat16),
-        in_specs=[pl.BlockSpec(memory_space=pltpu.VMEM)] * 3,
+        in_specs=[
+            pl.BlockSpec(memory_space=pltpu.VMEM),
+            pl.BlockSpec(memory_space=pl.ANY),
+            pl.BlockSpec(memory_space=pltpu.VMEM),
+        ],
         out_specs=pl.BlockSpec(memory_space=pltpu.VMEM),
         scratch_shapes=[
             pltpu.VMEM((n, rows, weight.shape[0]), jnp.bfloat16),
             pltpu.VMEM((tokens, features), jnp.bfloat16),
             pltpu.VMEM((m - 1, here, features), jnp.bfloat16),
+            pltpu.VMEM(weight.shape, jnp.bfloat16),
             dma((m - 1,)), dma((m - 1,)),
             dma((half - 1,)), dma((half - 1,)),
             dma((half,)), dma((half,)),
             dma((m - 1,)), dma((m - 1,)),
+            dma((1,)),
         ],
         compiler_params=pltpu.CompilerParams(
             collective_id=collective_id, has_side_effects=True, vmem_limit_bytes=VMEM_LIMIT

time: 300 us -> 282 us (0.940); the launches traced: 297 us -> 282 us
  Pallas kernels: 276 us -> 262 us
    pallas_call x3, Pallas kernels: 152 us -> 139 us  [project(): pl.pallas_call(functools.partial(project_kernel, n, m, tuple(blocks), sil...]
where the time goes in v2:
time: 282 us
  Pallas kernels  262 us (93%)
  local copies, waits for them, and re-layouts  20.1 us (7%)
    pallas_call x3, Pallas kernels, project(): pl.pallas_call(functools.partial(project_kernel, n, m, tuple(blocks), sil...  139 us
    pallas_call x3, Pallas kernels, output(): pl.pallas_call(functools.partial(output_kernel, n, m, regroup), out_shape...  104 us
    pallas_call x2, Pallas kernels, attend(): pl.pallas_call(functools.partial(attend_kernel, width // HEAD_DIM, own),...  18.3 us
    unnamed x1, local copies, waits for them, and re-layouts  12.6 us

profile of v2, /device:TPU:7, one launch (start us, length us, event | category | flops | bytes accessed | tf_op | source)
XLA Modules:
  0.0 282.0 jit_solution(7157484869836027789)
XLA Ops:
  0.0 0.7 broadcast_in_dim.9
  0.7 0.7 reshape_reshape.8.length_ref
  1.4 0.7 broadcast_in_dim.11
  2.1 0.7 reshape_reshape.9.length_ref
  2.8 1.4 fusion
  4.2 1.6 reshape.6.x_ref.res_ref
  5.8 43.2 %shard_map.136.q_ref = bf16[4,16,3072]{2,1,0:T(8,128)(2,1)} custom-call(bf16[128,512]{1,0:T(8,128)(2,1)} %reshape.6.x_ref.res_ref, f32[1,512]{1,0:T(1,128)} %get-tuple-element.6.gain_ref, bf16[3,512,1024]{2,1,0:T(8,128)(2,1)} %bitcast.6), custom_call_target="tpu_custom_call" | custom-call | tf_op jit(solution)/shard_map/pallas_call | solution.py:205
  49.0 7.4 %shard_map.137.a_ref = bf16[4,16,1024]{2,1,0:T(8,128)(2,1)} custom-call(bf16[4,16,3072]{2,1,0:T(8,128)(2,1)} %shard_map.136.q_ref, bf16[8,32,4096]{2,1,0:T(8,128)(2,1)} %k_ref.2, bf16[8,32,4096]{2,1,0:T(8,128)(2,1)} %v_ref.2, s32[16,1]{1,0:T(8,128)} %reshape_reshape.8.length_ref), custom_call_target="tpu_custom_call" | custom-call | tf_op jit(solution)/shard_map/pallas_call | solution.py:416
  56.4 29.2 %shard_map.138.x_ref.res_ref = bf16[128,512]{1,0:T(8,128)(2,1)} custom-call(bf16[4,16,1024]{2,1,0:T(8,128)(2,1)} %shard_map.137.a_ref, bf16[1024,512]{1,0:T(8,128)(2,1)} %w_ref.3, bf16[128,512]{1,0:T(8,128)(2,1)} %reshape.6.x_ref.res_ref), custom_call_target="tpu_custom_call" | custom-call | tf_op jit(solution)/shard_map/pallas_call | solution.py:342
  85.6 29.2 %shard_map.139.q_ref = bf16[4,16,1024]{2,1,0:T(8,128)(2,1)} custom-call(bf16[128,512]{1,0:T(8,128)(2,1)} %shard_map.138.x_ref.res_ref, f32[1,512]{1,0:T(1,128)} %get-tuple-element.7.gain_ref, bf16[1,512,1024]{2,1,0:T(8,128)(2,1)} %bitcast.7), custom_call_target="tpu_custom_call" | custom-call | tf_op jit(solution)/shard_map/pallas_call | solution.py:205
  114.8 11.0 %shard_map.140.a_ref = bf16[4,16,1024]{2,1,0:T(8,128)(2,1)} custom-call(bf16[4,16,1024]{2,1,0:T(8,128)(2,1)} %shard_map.139.q_ref, bf16[8,128,4096]{2,1,0:T(8,128)(2,1)} %k_ref.3, bf16[8,128,4096]{2,1,0:T(8,128)(2,1)} %v_ref.3, s32[16,1]{1,0:T(8,128)} %reshape_reshape.9.length_ref), custom_call_target="tpu_custom_call" | custom-call | tf_op jit(solution)/shard_map/pallas_call | solution.py:416
  125.7 29.7 %shard_map.141.x_ref.res_ref = bf16[128,512]{1,0:T(8,128)(2,1)} custom-call(bf16[4,16,1024]{2,1,0:T(8,128)(2,1)} %shard_map.140.a_ref, bf16[1024,512]{1,0:T(8,128)(2,1)} %w_ref.4, bf16[128,512]{1,0:T(8,128)(2,1)} %shard_map.138.x_ref.res_ref), custom_call_target="tpu_custom_call" | custom-call | tf_op jit(solution)/shard_map/pallas_call | solution.py:342
  155.5 12.6 %copy.22 = bf16[512,2,4096]{2,0,1:T(8,128)(2,1)} copy(bf16[512,2,4096]{2,1,0:T(2,128)(2,1)} %param.20) | data formatting | bytes 16777216 | tf_op args[6]
  168.1 66.9 %shard_map.142.a_ref = bf16[64,4096]{1,0:T(8,128)(2,1)} custom-call(bf16[128,512]{1,0:T(8,128)(2,1)} %shard_map.141.x_ref.res_ref, f32[1,512]{1,0:T(1,128)} %get-tuple-element.5.gain_ref, bf16[2,512,4096]{2,1,0:T(8,128)(2,1)} %bitcast.5), custom_call_target="tpu_custom_call" | custom-call | tf_op jit(solution)/shard_map/pallas_call | solution.py:205
  235.0 45.4 %shard_map.143 = bf16[128,512]{1,0:T(8,128)(2,1)} custom-call(bf16[64,4096]{1,0:T(8,128)(2,1)} %shard_map.142.a_ref, bf16[4096,512]{1,0:T(8,128)(2,1)} %w_ref.5, bf16[128,512]{1,0:T(8,128)(2,1)} %shard_map.141.x_ref.res_ref), custom_call_target="tpu_custom_call" | custom-call | tf_op jit(solution)/shard_map/pallas_call | solution.py:342
  280.4 1.6 reshape.7

commit v3 on v2

--- a/solution.py
+++ b/solution.py
@@ -110,6 +110,21 @@
         copy.start()
         pair.append(copy)
 
+    two_step = half == 4
+    beside = q + 1 - 2 * lax.rem(q, 2)
+    across = lax.rem(q + 2, 4)
+
+    def legs(b):
+        near, far = (beside, across) if b % 2 == 0 else (across, beside)
+        return ((near, near), (3 - q, near), (far, far))
+
+    def leg_copy(b, k, columns):
+        chunk, chip = legs(b)[k]
+        return remote(
+            mine.at[rows_at(chunk, rows), columns], arrived.at[k, :, columns],
+            cs.at[k, b], cr.at[k, b], (chip * 2 + c, g),
+        )
+
     cross = []
     for b, block in enumerate(blocks):
         _, _, width, at = block
@@ -119,6 +134,12 @@
         mine[:, columns] = (product + landed[:, columns].astype(jnp.float32)).astype(
             jnp.bfloat16
         )
+        if two_step:
+            for k in range(2):
+                copy = leg_copy(b, k, columns)
+                copy.start()
+                cross.append((b, k, copy))
+            continue
         for k in range(1, half):
             target = lax.rem(q + k, half)
             copy = remote(
@@ -128,6 +149,21 @@
             copy.start()
             cross.append((b, k, copy))
 
+    if two_step:
+        for b, block in enumerate(blocks):
+            _, _, width, at = block
+            columns = pl.ds(at, width)
+            for copy in (cross[2 * b][2], cross[2 * b + 1][2]):
+                copy.wait_recv()
+            onward = rows_at(legs(b)[2][0], rows)
+            mine[onward, columns] = (
+                mine[onward, columns].astype(jnp.float32)
+                + arrived[1, :, columns].astype(jnp.float32)
+            ).astype(jnp.bfloat16)
+            copy = leg_copy(b, 2, columns)
+            copy.start()
+            cross.append((b, 2, copy))
+
     n_columns = blocks[0][3]
     piece = rows // m
     away = []
@@ -135,11 +171,11 @@
         _, _, width, at = block
         columns = pl.ds(at, width)
         for bb, k, copy in cross:
-            if bb == b:
+            if bb == b and (k == 2 or not two_step):
                 copy.wait_recv()
         summed = mine[rows_at(q, rows), columns].astype(jnp.float32)
-        for k in range(1, half):
-            summed = summed + arrived[k - 1, :, columns].astype(jnp.float32)
+        for k in (0, 2) if two_step else range(half - 1):
+            summed = summed + arrived[k, :, columns].astype(jnp.float32)
         if b == 0:
             factor = lax.rsqrt(summed[:, 0:1] / D + EPSILON)
         elif silu:
@@ -188,8 +224,8 @@
     step = width
     while step > 1024 and step % 2 == 0:
         step //= 2
-    if parts == 1 and step == width and width % 512 == 0:
-        step = width // 2
+    if (parts * (width // step)) % 2 == 1 and step % 256 == 0:
+        step //= 2
     blocks = [
         (j, at, step, j * width + at) for j in range(parts) for at in range(0, width, step)
     ]

time: 282 us -> 269 us (0.954)
  Pallas kernels: 262 us -> 248 us
    pallas_call x3, Pallas kernels: 139 us -> 126 us  [project(): pl.pallas_call(functools.partial(project_kernel, n, m, tuple(blocks), sil...]
where the time goes in v3:
time: 269 us
  Pallas kernels  248 us (92%)
  local copies, waits for them, and re-layouts  20.1 us (7%)
    pallas_call x3, Pallas kernels, project(): pl.pallas_call(functools.partial(project_kernel, n, m, tuple(blocks), sil...  126 us
    pallas_call x3, Pallas kernels, output(): pl.pallas_call(functools.partial(output_kernel, n, m, regroup), out_shape...  104 us
    pallas_call x2, Pallas kernels, attend(): pl.pallas_call(functools.partial(attend_kernel, width // HEAD_DIM, own),...  18.3 us
    unnamed x1, local copies, waits for them, and re-layouts  12.6 us

profile of v3, /device:TPU:7, one launch (start us, length us, event | category | flops | bytes accessed | tf_op | source)
XLA Modules:
  0.0 268.6 jit_solution(635358492472932228)
XLA Ops:
  0.0 0.7 broadcast_in_dim.9
  0.7 0.7 reshape_reshape.8.length_ref
  1.4 0.7 broadcast_in_dim.11
  2.1 0.7 reshape_reshape.9.length_ref
  2.8 1.4 fusion
  4.2 1.6 reshape.6.x_ref.res_ref
  5.8 40.9 %shard_map.136.q_ref = bf16[4,16,3072]{2,1,0:T(8,128)(2,1)} custom-call(bf16[128,512]{1,0:T(8,128)(2,1)} %reshape.6.x_ref.res_ref, f32[1,512]{1,0:T(1,128)} %get-tuple-element.6.gain_ref, bf16[3,512,1024]{2,1,0:T(8,128)(2,1)} %bitcast.6), custom_call_target="tpu_custom_call" | custom-call | tf_op jit(solution)/shard_map/pallas_call | solution.py:241
  46.7 7.4 %shard_map.137.a_ref = bf16[4,16,1024]{2,1,0:T(8,128)(2,1)} custom-call(bf16[4,16,3072]{2,1,0:T(8,128)(2,1)} %shard_map.136.q_ref, bf16[8,32,4096]{2,1,0:T(8,128)(2,1)} %k_ref.2, bf16[8,32,4096]{2,1,0:T(8,128)(2,1)} %v_ref.2, s32[16,1]{1,0:T(8,128)} %reshape_reshape.8.length_ref), custom_call_target="tpu_custom_call" | custom-call | tf_op jit(solution)/shard_map/pallas_call | solution.py:452
  54.1 30.6 %shard_map.138.x_ref.res_ref = bf16[128,512]{1,0:T(8,128)(2,1)} custom-call(bf16[4,16,1024]{2,1,0:T(8,128)(2,1)} %shard_map.137.a_ref, bf16[1024,512]{1,0:T(8,128)(2,1)} %w_ref.3, bf16[128,512]{1,0:T(8,128)(2,1)} %reshape.6.x_ref.res_ref), custom_call_target="tpu_custom_call" | custom-call | tf_op jit(solution)/shard_map/pallas_call | solution.py:378
  84.7 29.7 %shard_map.139.q_ref = bf16[4,16,1024]{2,1,0:T(8,128)(2,1)} custom-call(bf16[128,512]{1,0:T(8,128)(2,1)} %shard_map.138.x_ref.res_ref, f32[1,512]{1,0:T(1,128)} %get-tuple-element.7.gain_ref, bf16[1,512,1024]{2,1,0:T(8,128)(2,1)} %bitcast.7), custom_call_target="tpu_custom_call" | custom-call | tf_op jit(solution)/shard_map/pallas_call | solution.py:241
  114.4 11.0 %shard_map.140.a_ref = bf16[4,16,1024]{2,1,0:T(8,128)(2,1)} custom-call(bf16[4,16,1024]{2,1,0:T(8,128)(2,1)} %shard_map.139.q_ref, bf16[8,128,4096]{2,1,0:T(8,128)(2,1)} %k_ref.3, bf16[8,128,4096]{2,1,0:T(8,128)(2,1)} %v_ref.3, s32[16,1]{1,0:T(8,128)} %reshape_reshape.9.length_ref), custom_call_target="tpu_custom_call" | custom-call | tf_op jit(solution)/shard_map/pallas_call | solution.py:452
  125.4 29.7 %shard_map.141.x_ref.res_ref = bf16[128,512]{1,0:T(8,128)(2,1)} custom-call(bf16[4,16,1024]{2,1,0:T(8,128)(2,1)} %shard_map.140.a_ref, bf16[1024,512]{1,0:T(8,128)(2,1)} %w_ref.4, bf16[128,512]{1,0:T(8,128)(2,1)} %shard_map.138.x_ref.res_ref), custom_call_target="tpu_custom_call" | custom-call | tf_op jit(solution)/shard_map/pallas_call | solution.py:378
  155.1 12.6 %copy.22 = bf16[512,2,4096]{2,0,1:T(8,128)(2,1)} copy(bf16[512,2,4096]{2,1,0:T(2,128)(2,1)} %param.20) | data formatting | bytes 16777216 | tf_op args[6]
  167.8 55.3 %shard_map.142.a_ref = bf16[64,4096]{1,0:T(8,128)(2,1)} custom-call(bf16[128,512]{1,0:T(8,128)(2,1)} %shard_map.141.x_ref.res_ref, f32[1,512]{1,0:T(1,128)} %get-tuple-element.5.gain_ref, bf16[2,512,4096]{2,1,0:T(8,128)(2,1)} %bitcast.5), custom_call_target="tpu_custom_call" | custom-call | tf_op jit(solution)/shard_map/pallas_call | solution.py:241
  223.0 43.9 %shard_map.143 = bf16[128,512]{1,0:T(8,128)(2,1)} custom-call(bf16[64,4096]{1,0:T(8,128)(2,1)} %shard_map.142.a_ref, bf16[4096,512]{1,0:T(8,128)(2,1)} %w_ref.5, bf16[128,512]{1,0:T(8,128)(2,1)} %shard_map.141.x_ref.res_ref), custom_call_target="tpu_custom_call" | custom-call | tf_op jit(solution)/shard_map/pallas_call | solution.py:378
  267.0 1.6 reshape.7
